TPU v7x, 32 devices: a whole 2x2x4 slice. The times are simulated.
32 devices in a mesh: mesh: 8 (over z, x), sub: 4 (over y, core).
Axes of the slice: x: 2, y: 2, z: 4, core: 2. Of those that a mesh axis runs over, the one named last changes fastest.
Arguments:
- conductivity: float32 [4, 32, 2, 64, 128], P('sub', 'mesh'), may hold values from 0.3 to 3
- footprint: int32 [8, 8], replicated, may hold values from 0 to 31, as said below
- initial: float32 [8, 8, 512, 128], P('mesh', 'sub'), may hold values from -30 to 30
- observed: float32 [8, 3, 8, 512, 128], P('mesh', None, 'sub'), may hold values from -6 to 6
Outputs:
- gradient: float32 [4, 32, 2, 64, 128], P('sub', 'mesh')
- last_field: float32 [8, 8, 512, 128], P('mesh', 'sub')
Inputs may be any that keep to these rules, and one draw needn't show every extreme that they name: `footprint`: each row names 8 different blocks; in every row, each range k * 4 to (k + 1) * 4 - 1 holds at most one of the row's ids.
All inputs are finite; a program needn't handle non-finite values.
Results may differ from a plain program's by a relative error of at most 0.00011.
Values sent between devices are 32-bit elements; how exact they have to be, the bound alone decides.
A program may use at most 128 MiB of HBM per device.

v0:
```python
import jax
import jax.numpy as jnp
from jax import lax
from jax.sharding import PartitionSpec as P

STEPS = 3
DEG = 6
low_bound = 0.3
high_bound = 15.0


def padded_2(x, sides, width):
    for axis, dim in sides:
        count, length = (lax.axis_size(axis), x.shape[dim])
        up = [(i, (i + 1) % count) for i in range(count - 1)]
        down = [(j, i) for i, j in up]
        last = lax.slice_in_dim(x, length - width, length, axis=dim)
        leading = lax.slice_in_dim(x, 0, width, axis=dim)
        before = lax.ppermute(last, axis, up)
        after = lax.ppermute(leading, axis, down)
        x = jnp.concatenate([before, x, after], axis=dim)
    return x


def halo_operator(field, conduct):
    padded = padded_2(field, (("sub", 0),), 1)
    padded = jnp.pad(padded, ((0, 0), (1, 1), (1, 1)))
    beside = padded[2:, 1:-1, 1:-1] + padded[:-2, 1:-1, 1:-1]
    beside = beside + padded[1:-1, 2:, 1:-1] + padded[1:-1, :-2, 1:-1]
    beside = beside + padded[1:-1, 1:-1, 2:] + padded[1:-1, 1:-1, :-2]
    return (6.0 + conduct) * field - beside


def chebyshev(source, conduct, operate):
    centre = (high_bound + low_bound) / 2.0
    half_width = (high_bound - low_bound) / 2.0
    ratio_now = half_width / centre
    direct = source / centre
    remain = source
    iterate = direct
    for repeat in range(DEG):
        remain = remain - operate(direct, conduct)
        ratio_next = 1.0 / (2.0 * centre / half_width - ratio_now)
        direct = ratio_next * ratio_now * direct + 2.0 * ratio_next / half_width * remain
        iterate = iterate + direct
        ratio_now = ratio_next
    return iterate


def one_mesh(conduct, start_field, observed_mesh, operate):
    fields = [start_field]
    for step in range(STEPS):
        fields.append(chebyshev(conduct * fields[-1], conduct, operate))
    adjoint = jnp.zeros_like(start_field)
    summed = jnp.zeros_like(start_field)
    for step in range(STEPS, 0, -1):
        adjoint = chebyshev(
            fields[step] - observed_mesh[step - 1] + conduct * adjoint, conduct, operate
        )
        summed = summed + adjoint * (fields[step - 1] - fields[step])
    return (fields[-1], summed)


def body(conductivity, footprint, initial, observed):
    my_index = lax.axis_index("mesh")
    per_owner = conductivity.shape[1]
    depth = conductivity.shape[2]
    block_y = conductivity.shape[3]
    across = conductivity.shape[4]
    tile_count = footprint.shape[1]
    cell_count = depth * block_y * across
    my_blocks = lax.dynamic_index_in_dim(footprint, my_index, 0, keepdims=False)
    shard_rows = lax.all_gather(conductivity, "mesh", axis=1, tiled=True)
    row_count = shard_rows.shape[1]
    flat_rows = shard_rows[0].reshape(row_count, cell_count)
    chosen = (my_blocks[:, None] == jnp.arange(row_count, dtype=jnp.int32)[None, :]).astype(
        jnp.float32
    )
    tile_values = jnp.dot(chosen, flat_rows, precision=lax.Precision.HIGHEST)
    conduct = jnp.transpose(
        tile_values.reshape(tile_count, depth, block_y, across), (1, 0, 2, 3)
    ).reshape(depth, tile_count * block_y, across)
    final_field, summed = one_mesh(conduct, initial[0], observed[0], halo_operator)
    grad_tiles = jnp.transpose(
        summed.reshape(depth, tile_count, block_y, across), (1, 0, 2, 3)
    ).reshape(tile_count, cell_count)
    chosen = (
        jnp.arange(per_owner * lax.axis_size("mesh"), dtype=jnp.int32)[:, None]
        == my_blocks[None, :]
    ).astype(jnp.float32)
    grad_rows = lax.psum_scatter(
        jnp.dot(chosen, grad_tiles, precision=lax.Precision.HIGHEST),
        "mesh",
        scatter_dimension=0,
        tiled=True,
    )
    gradient = grad_rows.reshape(1, per_owner, depth, block_y, across)
    return (gradient, final_field[None])


def solution(mesh):
    return jax.shard_map(
        body,
        mesh=mesh,
        in_specs=(
            P("sub", "mesh", None, None, None),
            P(),
            P("mesh", "sub", None, None),
            P("mesh", None, "sub", None, None),
        ),
        out_specs=(P("sub", "mesh", None, None, None), P("mesh", "sub", None, None)),
        check_vma=False,
    )
```

profile of v0, /device:TPU:0, one launch (start us, length us, event | category | flops | bytes accessed | tf_op | source)
XLA Modules:
  0.0 570.4 jit_solution(3698757126698177843)
XLA Ops:
  8.0 54.2 %all-gather.2.cloned.1.call-done = f32[1,32,2,64,128]{4,3,2,0,1:T(8,128)} async-done(((f32[1,4,2,64,128]{4,3,2,0,1:T(8,128)}), f32[1,32,2,64,128]{4,3,2,0,1:T(8,128)}) %all-gather.2.cloned.1.call-update) | async-done | bytes 2097168 | tf_op jit(solution)/shard_map/all_gather | solution.py:73
  85.0 7.2 %collective-permute-start.5 = (f32[1,512,128]{2,1,0:T(8,128)S(1)}, f32[1,512,128]{2,1,0:T(8,128)S(1)}, u32[]{:S(2)}, u32[]{:S(2)}) collective-permute-start(f32[1,512,128]{2,1,0:T(8,128)S(1)} %get-tuple-element.145), channel_id=1, source_target_pairs={{0,1},{1,2},{2,3},{4,5},{5,6},{6,7},{8,9},{9,10},{10,11},{12,13},{... | collective-permute-start | bytes 786440 | tf_op jit(solution)/shard_map/ppermute | solution.py:19
  95.9 7.2 %collective-permute-start.7 = (f32[1,512,128]{2,1,0:T(8,128)S(1)}, f32[1,512,128]{2,1,0:T(8,128)S(1)}, u32[]{:S(2)}, u32[]{:S(2)}) collective-permute-start(f32[1,512,128]{2,1,0:T(8,128)S(1)} %get-tuple-element.143), channel_id=1, source_target_pairs={{0,1},{1,2},{2,3},{4,5},{5,6},{6,7},{8,9},{9,10},{10,11},{12,13},{... | collective-permute-start | bytes 786440 | tf_op jit(solution)/shard_map/ppermute | solution.py:19
  106.7 7.2 %collective-permute-start.9 = (f32[1,512,128]{2,1,0:T(8,128)S(1)}, f32[1,512,128]{2,1,0:T(8,128)S(1)}, u32[]{:S(2)}, u32[]{:S(2)}) collective-permute-start(f32[1,512,128]{2,1,0:T(8,128)S(1)} %get-tuple-element.141), channel_id=1, source_target_pairs={{0,1},{1,2},{2,3},{4,5},{5,6},{6,7},{8,9},{9,10},{10,11},{12,13},{... | collective-permute-start | bytes 786440 | tf_op jit(solution)/shard_map/ppermute | solution.py:19
  117.5 7.4 %collective-permute-start.11 = (f32[1,512,128]{2,1,0:T(8,128)S(1)}, f32[1,512,128]{2,1,0:T(8,128)S(1)}, u32[]{:S(2)}, u32[]{:S(2)}) collective-permute-start(f32[1,512,128]{2,1,0:T(8,128)S(1)} %get-tuple-element.139), channel_id=1, source_target_pairs={{0,1},{1,2},{2,3},{4,5},{5,6},{6,7},{8,9},{9,10},{10,11},{12,13},{... | collective-permute-start | bytes 786440 | tf_op jit(solution)/shard_map/ppermute | solution.py:19
  128.5 7.2 %collective-permute-start.13 = (f32[1,512,128]{2,1,0:T(8,128)S(1)}, f32[1,512,128]{2,1,0:T(8,128)S(1)}, u32[]{:S(2)}, u32[]{:S(2)}) collective-permute-start(f32[1,512,128]{2,1,0:T(8,128)S(1)} %get-tuple-element.137), channel_id=1, source_target_pairs={{0,1},{1,2},{2,3},{4,5},{5,6},{6,7},{8,9},{9,10},{10,11},{12,13},{... | collective-permute-start | bytes 786440 | tf_op jit(solution)/shard_map/ppermute | solution.py:19
  139.3 7.2 %collective-permute-start.15 = (f32[1,512,128]{2,1,0:T(8,128)S(1)}, f32[1,512,128]{2,1,0:T(8,128)S(1)}, u32[]{:S(2)}, u32[]{:S(2)}) collective-permute-start(f32[1,512,128]{2,1,0:T(8,128)S(1)} %get-tuple-element.135), channel_id=1, source_target_pairs={{0,1},{1,2},{2,3},{4,5},{5,6},{6,7},{8,9},{9,10},{10,11},{12,13},{... | collective-permute-start | bytes 786440 | tf_op jit(solution)/shard_map/ppermute | solution.py:19
  150.1 7.2 %collective-permute-start.17 = (f32[1,512,128]{2,1,0:T(8,128)S(1)}, f32[1,512,128]{2,1,0:T(8,128)S(1)}, u32[]{:S(2)}, u32[]{:S(2)}) collective-permute-start(f32[1,512,128]{2,1,0:T(8,128)S(1)} %get-tuple-element.133), channel_id=1, source_target_pairs={{0,1},{1,2},{2,3},{4,5},{5,6},{6,7},{8,9},{9,10},{10,11},{12,13},{... | collective-permute-start | bytes 786440 | tf_op jit(solution)/shard_map/ppermute | solution.py:19
  160.9 7.2 %collective-permute-start.19 = (f32[1,512,128]{2,1,0:T(8,128)S(1)}, f32[1,512,128]{2,1,0:T(8,128)S(1)}, u32[]{:S(2)}, u32[]{:S(2)}) collective-permute-start(f32[1,512,128]{2,1,0:T(8,128)S(1)} %get-tuple-element.131), channel_id=1, source_target_pairs={{0,1},{1,2},{2,3},{4,5},{5,6},{6,7},{8,9},{9,10},{10,11},{12,13},{... | collective-permute-start | bytes 786440 | tf_op jit(solution)/shard_map/ppermute | solution.py:19
  171.8 7.2 %collective-permute-start.21 = (f32[1,512,128]{2,1,0:T(8,128)S(1)}, f32[1,512,128]{2,1,0:T(8,128)S(1)}, u32[]{:S(2)}, u32[]{:S(2)}) collective-permute-start(f32[1,512,128]{2,1,0:T(8,128)S(1)} %get-tuple-element.129), channel_id=1, source_target_pairs={{0,1},{1,2},{2,3},{4,5},{5,6},{6,7},{8,9},{9,10},{10,11},{12,13},{... | collective-permute-start | bytes 786440 | tf_op jit(solution)/shard_map/ppermute | solution.py:19
  182.6 7.2 %collective-permute-start.23 = (f32[1,512,128]{2,1,0:T(8,128)S(1)}, f32[1,512,128]{2,1,0:T(8,128)S(1)}, u32[]{:S(2)}, u32[]{:S(2)}) collective-permute-start(f32[1,512,128]{2,1,0:T(8,128)S(1)} %get-tuple-element.127), channel_id=1, source_target_pairs={{0,1},{1,2},{2,3},{4,5},{5,6},{6,7},{8,9},{9,10},{10,11},{12,13},{... | collective-permute-start | bytes 786440 | tf_op jit(solution)/shard_map/ppermute | solution.py:19
  193.6 7.2 %collective-permute-start.25 = (f32[1,512,128]{2,1,0:T(8,128)S(1)}, f32[1,512,128]{2,1,0:T(8,128)S(1)}, u32[]{:S(2)}, u32[]{:S(2)}) collective-permute-start(f32[1,512,128]{2,1,0:T(8,128)S(1)} %get-tuple-element.125), channel_id=1, source_target_pairs={{0,1},{1,2},{2,3},{4,5},{5,6},{6,7},{8,9},{9,10},{10,11},{12,13},{... | collective-permute-start | bytes 786440 | tf_op jit(solution)/shard_map/ppermute | solution.py:19
  204.4 7.4 %collective-permute-start.27 = (f32[1,512,128]{2,1,0:T(8,128)S(1)}, f32[1,512,128]{2,1,0:T(8,128)S(1)}, u32[]{:S(2)}, u32[]{:S(2)}) collective-permute-start(f32[1,512,128]{2,1,0:T(8,128)S(1)} %get-tuple-element.123), channel_id=1, source_target_pairs={{0,1},{1,2},{2,3},{4,5},{5,6},{6,7},{8,9},{9,10},{10,11},{12,13},{... | collective-permute-start | bytes 786440 | tf_op jit(solution)/shard_map/ppermute | solution.py:19
  215.2 7.2 %collective-permute-start.29 = (f32[1,512,128]{2,1,0:T(8,128)S(1)}, f32[1,512,128]{2,1,0:T(8,128)S(1)}, u32[]{:S(2)}, u32[]{:S(2)}) collective-permute-start(f32[1,512,128]{2,1,0:T(8,128)S(1)} %get-tuple-element.121), channel_id=1, source_target_pairs={{0,1},{1,2},{2,3},{4,5},{5,6},{6,7},{8,9},{9,10},{10,11},{12,13},{... | collective-permute-start | bytes 786440 | tf_op jit(solution)/shard_map/ppermute | solution.py:19
  226.1 7.2 %collective-permute-start.31 = (f32[1,512,128]{2,1,0:T(8,128)S(1)}, f32[1,512,128]{2,1,0:T(8,128)S(1)}, u32[]{:S(2)}, u32[]{:S(2)}) collective-permute-start(f32[1,512,128]{2,1,0:T(8,128)S(1)} %get-tuple-element.119), channel_id=1, source_target_pairs={{0,1},{1,2},{2,3},{4,5},{5,6},{6,7},{8,9},{9,10},{10,11},{12,13},{... | collective-permute-start | bytes 786440 | tf_op jit(solution)/shard_map/ppermute | solution.py:19
  236.9 7.2 %collective-permute-start.33 = (f32[1,512,128]{2,1,0:T(8,128)S(1)}, f32[1,512,128]{2,1,0:T(8,128)S(1)}, u32[]{:S(2)}, u32[]{:S(2)}) collective-permute-start(f32[1,512,128]{2,1,0:T(8,128)S(1)} %get-tuple-element.117), channel_id=1, source_target_pairs={{0,1},{1,2},{2,3},{4,5},{5,6},{6,7},{8,9},{9,10},{10,11},{12,13},{... | collective-permute-start | bytes 786440 | tf_op jit(solution)/shard_map/ppermute | solution.py:19
  247.8 7.2 %collective-permute-start.35 = (f32[1,512,128]{2,1,0:T(8,128)S(1)}, f32[1,512,128]{2,1,0:T(8,128)S(1)}, u32[]{:S(2)}, u32[]{:S(2)}) collective-permute-start(f32[1,512,128]{2,1,0:T(8,128)S(1)} %get-tuple-element.115), channel_id=1, source_target_pairs={{0,1},{1,2},{2,3},{4,5},{5,6},{6,7},{8,9},{9,10},{10,11},{12,13},{... | collective-permute-start | bytes 786440 | tf_op jit(solution)/shard_map/ppermute | solution.py:19
  258.8 7.2 %collective-permute-start.37 = (f32[1,512,128]{2,1,0:T(8,128)S(1)}, f32[1,512,128]{2,1,0:T(8,128)S(1)}, u32[]{:S(2)}, u32[]{:S(2)}) collective-permute-start(f32[1,512,128]{2,1,0:T(8,128)S(1)} %get-tuple-element.113), channel_id=1, source_target_pairs={{0,1},{1,2},{2,3},{4,5},{5,6},{6,7},{8,9},{9,10},{10,11},{12,13},{... | collective-permute-start | bytes 786440 | tf_op jit(solution)/shard_map/ppermute | solution.py:19
  269.7 7.2 %collective-permute-start.39 = (f32[1,512,128]{2,1,0:T(8,128)S(1)}, f32[1,512,128]{2,1,0:T(8,128)S(1)}, u32[]{:S(2)}, u32[]{:S(2)}) collective-permute-start(f32[1,512,128]{2,1,0:T(8,128)S(1)} %get-tuple-element.111), channel_id=1, source_target_pairs={{0,1},{1,2},{2,3},{4,5},{5,6},{6,7},{8,9},{9,10},{10,11},{12,13},{... | collective-permute-start | bytes 786440 | tf_op jit(solution)/shard_map/ppermute | solution.py:19
  280.5 7.2 %collective-permute-start.41 = (f32[1,512,128]{2,1,0:T(8,128)S(1)}, f32[1,512,128]{2,1,0:T(8,128)S(1)}, u32[]{:S(2)}, u32[]{:S(2)}) collective-permute-start(f32[1,512,128]{2,1,0:T(8,128)S(1)} %get-tuple-element.109), channel_id=1, source_target_pairs={{0,1},{1,2},{2,3},{4,5},{5,6},{6,7},{8,9},{9,10},{10,11},{12,13},{... | collective-permute-start | bytes 786440 | tf_op jit(solution)/shard_map/ppermute | solution.py:19
  291.3 7.6 %collective-permute-start.43 = (f32[1,512,128]{2,1,0:T(8,128)S(1)}, f32[1,512,128]{2,1,0:T(8,128)S(1)}, u32[]{:S(2)}, u32[]{:S(2)}) collective-permute-start(f32[1,512,128]{2,1,0:T(8,128)S(1)} %get-tuple-element.107), channel_id=1, source_target_pairs={{0,1},{1,2},{2,3},{4,5},{5,6},{6,7},{8,9},{9,10},{10,11},{12,13},{... | collective-permute-start | bytes 786440 | tf_op jit(solution)/shard_map/ppermute | solution.py:19
  302.1 7.2 %collective-permute-start.45 = (f32[1,512,128]{2,1,0:T(8,128)S(1)}, f32[1,512,128]{2,1,0:T(8,128)S(1)}, u32[]{:S(2)}, u32[]{:S(2)}) collective-permute-start(f32[1,512,128]{2,1,0:T(8,128)S(1)} %get-tuple-element.105), channel_id=1, source_target_pairs={{0,1},{1,2},{2,3},{4,5},{5,6},{6,7},{8,9},{9,10},{10,11},{12,13},{... | collective-permute-start | bytes 786440 | tf_op jit(solution)/shard_map/ppermute | solution.py:19
  312.9 7.2 %collective-permute-start.47 = (f32[1,512,128]{2,1,0:T(8,128)S(1)}, f32[1,512,128]{2,1,0:T(8,128)S(1)}, u32[]{:S(2)}, u32[]{:S(2)}) collective-permute-start(f32[1,512,128]{2,1,0:T(8,128)S(1)} %get-tuple-element.103), channel_id=1, source_target_pairs={{0,1},{1,2},{2,3},{4,5},{5,6},{6,7},{8,9},{9,10},{10,11},{12,13},{... | collective-permute-start | bytes 786440 | tf_op jit(solution)/shard_map/ppermute | solution.py:19
  324.0 7.2 %collective-permute-start.49 = (f32[1,512,128]{2,1,0:T(8,128)S(1)}, f32[1,512,128]{2,1,0:T(8,128)S(1)}, u32[]{:S(2)}, u32[]{:S(2)}) collective-permute-start(f32[1,512,128]{2,1,0:T(8,128)S(1)} %get-tuple-element.101), channel_id=1, source_target_pairs={{0,1},{1,2},{2,3},{4,5},{5,6},{6,7},{8,9},{9,10},{10,11},{12,13},{... | collective-permute-start | bytes 786440 | tf_op jit(solution)/shard_map/ppermute | solution.py:19
  334.8 7.2 %collective-permute-start.51 = (f32[1,512,128]{2,1,0:T(8,128)S(1)}, f32[1,512,128]{2,1,0:T(8,128)S(1)}, u32[]{:S(2)}, u32[]{:S(2)}) collective-permute-start(f32[1,512,128]{2,1,0:T(8,128)S(1)} %get-tuple-element.99), channel_id=1, source_target_pairs={{0,1},{1,2},{2,3},{4,5},{5,6},{6,7},{8,9},{9,10},{10,11},{12,13},{... | collective-permute-start | bytes 786440 | tf_op jit(solution)/shard_map/ppermute | solution.py:19
  345.6 7.2 %collective-permute-start.53 = (f32[1,512,128]{2,1,0:T(8,128)S(1)}, f32[1,512,128]{2,1,0:T(8,128)S(1)}, u32[]{:S(2)}, u32[]{:S(2)}) collective-permute-start(f32[1,512,128]{2,1,0:T(8,128)S(1)} %get-tuple-element.97), channel_id=1, source_target_pairs={{0,1},{1,2},{2,3},{4,5},{5,6},{6,7},{8,9},{9,10},{10,11},{12,13},{... | collective-permute-start | bytes 786440 | tf_op jit(solution)/shard_map/ppermute | solution.py:19
  356.4 7.2 %collective-permute-start.55 = (f32[1,512,128]{2,1,0:T(8,128)S(1)}, f32[1,512,128]{2,1,0:T(8,128)S(1)}, u32[]{:S(2)}, u32[]{:S(2)}) collective-permute-start(f32[1,512,128]{2,1,0:T(8,128)S(1)} %get-tuple-element.95), channel_id=1, source_target_pairs={{0,1},{1,2},{2,3},{4,5},{5,6},{6,7},{8,9},{9,10},{10,11},{12,13},{... | collective-permute-start | bytes 786440 | tf_op jit(solution)/shard_map/ppermute | solution.py:19
  367.2 7.2 %collective-permute-start.57 = (f32[1,512,128]{2,1,0:T(8,128)S(1)}, f32[1,512,128]{2,1,0:T(8,128)S(1)}, u32[]{:S(2)}, u32[]{:S(2)}) collective-permute-start(f32[1,512,128]{2,1,0:T(8,128)S(1)} %get-tuple-element.93), channel_id=1, source_target_pairs={{0,1},{1,2},{2,3},{4,5},{5,6},{6,7},{8,9},{9,10},{10,11},{12,13},{... | collective-permute-start | bytes 786440 | tf_op jit(solution)/shard_map/ppermute | solution.py:19
  378.0 7.4 %collective-permute-start.59 = (f32[1,512,128]{2,1,0:T(8,128)S(1)}, f32[1,512,128]{2,1,0:T(8,128)S(1)}, u32[]{:S(2)}, u32[]{:S(2)}) collective-permute-start(f32[1,512,128]{2,1,0:T(8,128)S(1)} %get-tuple-element.91), channel_id=1, source_target_pairs={{0,1},{1,2},{2,3},{4,5},{5,6},{6,7},{8,9},{9,10},{10,11},{12,13},{... | collective-permute-start | bytes 786440 | tf_op jit(solution)/shard_map/ppermute | solution.py:19
  389.1 7.2 %collective-permute-start.61 = (f32[1,512,128]{2,1,0:T(8,128)S(1)}, f32[1,512,128]{2,1,0:T(8,128)S(1)}, u32[]{:S(2)}, u32[]{:S(2)}) collective-permute-start(f32[1,512,128]{2,1,0:T(8,128)S(1)} %get-tuple-element.89), channel_id=1, source_target_pairs={{0,1},{1,2},{2,3},{4,5},{5,6},{6,7},{8,9},{9,10},{10,11},{12,13},{... | collective-permute-start | bytes 786440 | tf_op jit(solution)/shard_map/ppermute | solution.py:19
  432.3 7.2 %collective-permute-start.69 = (f32[1,512,128]{2,1,0:T(8,128)S(1)}, f32[1,512,128]{2,1,0:T(8,128)S(1)}, u32[]{:S(2)}, u32[]{:S(2)}) collective-permute-start(f32[1,512,128]{2,1,0:T(8,128)S(1)} %get-tuple-element.81), channel_id=1, source_target_pairs={{0,1},{1,2},{2,3},{4,5},{5,6},{6,7},{8,9},{9,10},{10,11},{12,13},{... | collective-permute-start | bytes 786440 | tf_op jit(solution)/shard_map/ppermute | solution.py:19
  456.7 104.8 %all-reduce.39.cloned.1.call-done = f32[32,16384]{1,0:T(8,128)} async-done(((f32[32,16384]{1,0:T(8,128)}), f32[32,16384]{1,0:T(8,128)}) %all-reduce.39.cloned.1.call-update) | async-done | bytes 2097168
  (249 shorter events, 178.3 us)
Async XLA Ops:
  7.2 55.0 %all-gather.2.cloned.1.call-start = ((), (), s32[]{:S(2)}) async-start(), calls=%async_computation | async-start | bytes 2359296 | tf_op jit(solution)/shard_map/all_gather | solution.py:73
  7.9 553.6 %all-reduce.39.cloned.1.call-start = ((), (), s32[]{:S(2)}) async-start(), calls=%async_computation.1 | async-start | bytes 4194304
  83.7 8.5 %collective-permute-start.4 = (f32[1,512,128]{2,1,0:T(8,128)S(1)}, f32[1,512,128]{2,1,0:T(8,128)S(1)}, u32[]{:S(2)}, u32[]{:S(2)}) collective-permute-start(f32[1,512,128]{2,1,0:T(8,128)S(1)} %get-tuple-element.146), channel_id=1, source_target_pairs={{1,0},{2,1},{3,2},{5,4},{6,5},{7,6},{9,8},{10,9},{11,10},{13,12},{... | collective-permute-start | bytes 786440 | tf_op jit(solution)/shard_map/ppermute | solution.py:20
  94.6 8.5 %collective-permute-start.6 = (f32[1,512,128]{2,1,0:T(8,128)S(1)}, f32[1,512,128]{2,1,0:T(8,128)S(1)}, u32[]{:S(2)}, u32[]{:S(2)}) collective-permute-start(f32[1,512,128]{2,1,0:T(8,128)S(1)} %get-tuple-element.144), channel_id=1, source_target_pairs={{1,0},{2,1},{3,2},{5,4},{6,5},{7,6},{9,8},{10,9},{11,10},{13,12},{... | collective-permute-start | bytes 786440 | tf_op jit(solution)/shard_map/ppermute | solution.py:20
  105.4 8.5 %collective-permute-start.8 = (f32[1,512,128]{2,1,0:T(8,128)S(1)}, f32[1,512,128]{2,1,0:T(8,128)S(1)}, u32[]{:S(2)}, u32[]{:S(2)}) collective-permute-start(f32[1,512,128]{2,1,0:T(8,128)S(1)} %get-tuple-element.142), channel_id=1, source_target_pairs={{1,0},{2,1},{3,2},{5,4},{6,5},{7,6},{9,8},{10,9},{11,10},{13,12},{... | collective-permute-start | bytes 786440 | tf_op jit(solution)/shard_map/ppermute | solution.py:20
  116.2 8.7 %collective-permute-start.10 = (f32[1,512,128]{2,1,0:T(8,128)S(1)}, f32[1,512,128]{2,1,0:T(8,128)S(1)}, u32[]{:S(2)}, u32[]{:S(2)}) collective-permute-start(f32[1,512,128]{2,1,0:T(8,128)S(1)} %get-tuple-element.140), channel_id=1, source_target_pairs={{1,0},{2,1},{3,2},{5,4},{6,5},{7,6},{9,8},{10,9},{11,10},{13,12},{... | collective-permute-start | bytes 786440 | tf_op jit(solution)/shard_map/ppermute | solution.py:20
  127.2 8.5 %collective-permute-start.12 = (f32[1,512,128]{2,1,0:T(8,128)S(1)}, f32[1,512,128]{2,1,0:T(8,128)S(1)}, u32[]{:S(2)}, u32[]{:S(2)}) collective-permute-start(f32[1,512,128]{2,1,0:T(8,128)S(1)} %get-tuple-element.138), channel_id=1, source_target_pairs={{1,0},{2,1},{3,2},{5,4},{6,5},{7,6},{9,8},{10,9},{11,10},{13,12},{... | collective-permute-start | bytes 786440 | tf_op jit(solution)/shard_map/ppermute | solution.py:20
  138.0 8.5 %collective-permute-start.14 = (f32[1,512,128]{2,1,0:T(8,128)S(1)}, f32[1,512,128]{2,1,0:T(8,128)S(1)}, u32[]{:S(2)}, u32[]{:S(2)}) collective-permute-start(f32[1,512,128]{2,1,0:T(8,128)S(1)} %get-tuple-element.136), channel_id=1, source_target_pairs={{1,0},{2,1},{3,2},{5,4},{6,5},{7,6},{9,8},{10,9},{11,10},{13,12},{... | collective-permute-start | bytes 786440 | tf_op jit(solution)/shard_map/ppermute | solution.py:20
  148.8 8.5 %collective-permute-start.16 = (f32[1,512,128]{2,1,0:T(8,128)S(1)}, f32[1,512,128]{2,1,0:T(8,128)S(1)}, u32[]{:S(2)}, u32[]{:S(2)}) collective-permute-start(f32[1,512,128]{2,1,0:T(8,128)S(1)} %get-tuple-element.134), channel_id=1, source_target_pairs={{1,0},{2,1},{3,2},{5,4},{6,5},{7,6},{9,8},{10,9},{11,10},{13,12},{... | collective-permute-start | bytes 786440 | tf_op jit(solution)/shard_map/ppermute | solution.py:20
  159.6 8.5 %collective-permute-start.18 = (f32[1,512,128]{2,1,0:T(8,128)S(1)}, f32[1,512,128]{2,1,0:T(8,128)S(1)}, u32[]{:S(2)}, u32[]{:S(2)}) collective-permute-start(f32[1,512,128]{2,1,0:T(8,128)S(1)} %get-tuple-element.132), channel_id=1, source_target_pairs={{1,0},{2,1},{3,2},{5,4},{6,5},{7,6},{9,8},{10,9},{11,10},{13,12},{... | collective-permute-start | bytes 786440 | tf_op jit(solution)/shard_map/ppermute | solution.py:20
  170.5 8.5 %collective-permute-start.20 = (f32[1,512,128]{2,1,0:T(8,128)S(1)}, f32[1,512,128]{2,1,0:T(8,128)S(1)}, u32[]{:S(2)}, u32[]{:S(2)}) collective-permute-start(f32[1,512,128]{2,1,0:T(8,128)S(1)} %get-tuple-element.130), channel_id=1, source_target_pairs={{1,0},{2,1},{3,2},{5,4},{6,5},{7,6},{9,8},{10,9},{11,10},{13,12},{... | collective-permute-start | bytes 786440 | tf_op jit(solution)/shard_map/ppermute | solution.py:20
  181.3 8.5 %collective-permute-start.22 = (f32[1,512,128]{2,1,0:T(8,128)S(1)}, f32[1,512,128]{2,1,0:T(8,128)S(1)}, u32[]{:S(2)}, u32[]{:S(2)}) collective-permute-start(f32[1,512,128]{2,1,0:T(8,128)S(1)} %get-tuple-element.128), channel_id=1, source_target_pairs={{1,0},{2,1},{3,2},{5,4},{6,5},{7,6},{9,8},{10,9},{11,10},{13,12},{... | collective-permute-start | bytes 786440 | tf_op jit(solution)/shard_map/ppermute | solution.py:20
  192.3 8.5 %collective-permute-start.24 = (f32[1,512,128]{2,1,0:T(8,128)S(1)}, f32[1,512,128]{2,1,0:T(8,128)S(1)}, u32[]{:S(2)}, u32[]{:S(2)}) collective-permute-start(f32[1,512,128]{2,1,0:T(8,128)S(1)} %get-tuple-element.126), channel_id=1, source_target_pairs={{1,0},{2,1},{3,2},{5,4},{6,5},{7,6},{9,8},{10,9},{11,10},{13,12},{... | collective-permute-start | bytes 786440 | tf_op jit(solution)/shard_map/ppermute | solution.py:20
  203.1 8.7 %collective-permute-start.26 = (f32[1,512,128]{2,1,0:T(8,128)S(1)}, f32[1,512,128]{2,1,0:T(8,128)S(1)}, u32[]{:S(2)}, u32[]{:S(2)}) collective-permute-start(f32[1,512,128]{2,1,0:T(8,128)S(1)} %get-tuple-element.124), channel_id=1, source_target_pairs={{1,0},{2,1},{3,2},{5,4},{6,5},{7,6},{9,8},{10,9},{11,10},{13,12},{... | collective-permute-start | bytes 786440 | tf_op jit(solution)/shard_map/ppermute | solution.py:20
  213.9 8.5 %collective-permute-start.28 = (f32[1,512,128]{2,1,0:T(8,128)S(1)}, f32[1,512,128]{2,1,0:T(8,128)S(1)}, u32[]{:S(2)}, u32[]{:S(2)}) collective-permute-start(f32[1,512,128]{2,1,0:T(8,128)S(1)} %get-tuple-element.122), channel_id=1, source_target_pairs={{1,0},{2,1},{3,2},{5,4},{6,5},{7,6},{9,8},{10,9},{11,10},{13,12},{... | collective-permute-start | bytes 786440 | tf_op jit(solution)/shard_map/ppermute | solution.py:20
  224.8 8.5 %collective-permute-start.30 = (f32[1,512,128]{2,1,0:T(8,128)S(1)}, f32[1,512,128]{2,1,0:T(8,128)S(1)}, u32[]{:S(2)}, u32[]{:S(2)}) collective-permute-start(f32[1,512,128]{2,1,0:T(8,128)S(1)} %get-tuple-element.120), channel_id=1, source_target_pairs={{1,0},{2,1},{3,2},{5,4},{6,5},{7,6},{9,8},{10,9},{11,10},{13,12},{... | collective-permute-start | bytes 786440 | tf_op jit(solution)/shard_map/ppermute | solution.py:20
  235.6 8.5 %collective-permute-start.32 = (f32[1,512,128]{2,1,0:T(8,128)S(1)}, f32[1,512,128]{2,1,0:T(8,128)S(1)}, u32[]{:S(2)}, u32[]{:S(2)}) collective-permute-start(f32[1,512,128]{2,1,0:T(8,128)S(1)} %get-tuple-element.118), channel_id=1, source_target_pairs={{1,0},{2,1},{3,2},{5,4},{6,5},{7,6},{9,8},{10,9},{11,10},{13,12},{... | collective-permute-start | bytes 786440 | tf_op jit(solution)/shard_map/ppermute | solution.py:20
  246.4 8.6 %collective-permute-start.34 = (f32[1,512,128]{2,1,0:T(8,128)S(1)}, f32[1,512,128]{2,1,0:T(8,128)S(1)}, u32[]{:S(2)}, u32[]{:S(2)}) collective-permute-start(f32[1,512,128]{2,1,0:T(8,128)S(1)} %get-tuple-element.116), channel_id=1, source_target_pairs={{1,0},{2,1},{3,2},{5,4},{6,5},{7,6},{9,8},{10,9},{11,10},{13,12},{... | collective-permute-start | bytes 786440 | tf_op jit(solution)/shard_map/ppermute | solution.py:20
  257.5 8.5 %collective-permute-start.36 = (f32[1,512,128]{2,1,0:T(8,128)S(1)}, f32[1,512,128]{2,1,0:T(8,128)S(1)}, u32[]{:S(2)}, u32[]{:S(2)}) collective-permute-start(f32[1,512,128]{2,1,0:T(8,128)S(1)} %get-tuple-element.114), channel_id=1, source_target_pairs={{1,0},{2,1},{3,2},{5,4},{6,5},{7,6},{9,8},{10,9},{11,10},{13,12},{... | collective-permute-start | bytes 786440 | tf_op jit(solution)/shard_map/ppermute | solution.py:20
  268.4 8.5 %collective-permute-start.38 = (f32[1,512,128]{2,1,0:T(8,128)S(1)}, f32[1,512,128]{2,1,0:T(8,128)S(1)}, u32[]{:S(2)}, u32[]{:S(2)}) collective-permute-start(f32[1,512,128]{2,1,0:T(8,128)S(1)} %get-tuple-element.112), channel_id=1, source_target_pairs={{1,0},{2,1},{3,2},{5,4},{6,5},{7,6},{9,8},{10,9},{11,10},{13,12},{... | collective-permute-start | bytes 786440 | tf_op jit(solution)/shard_map/ppermute | solution.py:20
  279.2 8.5 %collective-permute-start.40 = (f32[1,512,128]{2,1,0:T(8,128)S(1)}, f32[1,512,128]{2,1,0:T(8,128)S(1)}, u32[]{:S(2)}, u32[]{:S(2)}) collective-permute-start(f32[1,512,128]{2,1,0:T(8,128)S(1)} %get-tuple-element.110), channel_id=1, source_target_pairs={{1,0},{2,1},{3,2},{5,4},{6,5},{7,6},{9,8},{10,9},{11,10},{13,12},{... | collective-permute-start | bytes 786440 | tf_op jit(solution)/shard_map/ppermute | solution.py:20
  290.0 8.9 %collective-permute-start.42 = (f32[1,512,128]{2,1,0:T(8,128)S(1)}, f32[1,512,128]{2,1,0:T(8,128)S(1)}, u32[]{:S(2)}, u32[]{:S(2)}) collective-permute-start(f32[1,512,128]{2,1,0:T(8,128)S(1)} %get-tuple-element.108), channel_id=1, source_target_pairs={{1,0},{2,1},{3,2},{5,4},{6,5},{7,6},{9,8},{10,9},{11,10},{13,12},{... | collective-permute-start | bytes 786440 | tf_op jit(solution)/shard_map/ppermute | solution.py:20
  300.8 8.5 %collective-permute-start.44 = (f32[1,512,128]{2,1,0:T(8,128)S(1)}, f32[1,512,128]{2,1,0:T(8,128)S(1)}, u32[]{:S(2)}, u32[]{:S(2)}) collective-permute-start(f32[1,512,128]{2,1,0:T(8,128)S(1)} %get-tuple-element.106), channel_id=1, source_target_pairs={{1,0},{2,1},{3,2},{5,4},{6,5},{7,6},{9,8},{10,9},{11,10},{13,12},{... | collective-permute-start | bytes 786440 | tf_op jit(solution)/shard_map/ppermute | solution.py:20
  311.6 8.5 %collective-permute-start.46 = (f32[1,512,128]{2,1,0:T(8,128)S(1)}, f32[1,512,128]{2,1,0:T(8,128)S(1)}, u32[]{:S(2)}, u32[]{:S(2)}) collective-permute-start(f32[1,512,128]{2,1,0:T(8,128)S(1)} %get-tuple-element.104), channel_id=1, source_target_pairs={{1,0},{2,1},{3,2},{5,4},{6,5},{7,6},{9,8},{10,9},{11,10},{13,12},{... | collective-permute-start | bytes 786440 | tf_op jit(solution)/shard_map/ppermute | solution.py:20
  322.7 8.5 %collective-permute-start.48 = (f32[1,512,128]{2,1,0:T(8,128)S(1)}, f32[1,512,128]{2,1,0:T(8,128)S(1)}, u32[]{:S(2)}, u32[]{:S(2)}) collective-permute-start(f32[1,512,128]{2,1,0:T(8,128)S(1)} %get-tuple-element.102), channel_id=1, source_target_pairs={{1,0},{2,1},{3,2},{5,4},{6,5},{7,6},{9,8},{10,9},{11,10},{13,12},{... | collective-permute-start | bytes 786440 | tf_op jit(solution)/shard_map/ppermute | solution.py:20
  333.5 8.5 %collective-permute-start.50 = (f32[1,512,128]{2,1,0:T(8,128)S(1)}, f32[1,512,128]{2,1,0:T(8,128)S(1)}, u32[]{:S(2)}, u32[]{:S(2)}) collective-permute-start(f32[1,512,128]{2,1,0:T(8,128)S(1)} %get-tuple-element.100), channel_id=1, source_target_pairs={{1,0},{2,1},{3,2},{5,4},{6,5},{7,6},{9,8},{10,9},{11,10},{13,12},{... | collective-permute-start | bytes 786440 | tf_op jit(solution)/shard_map/ppermute | solution.py:20
  344.3 8.5 %collective-permute-start.52 = (f32[1,512,128]{2,1,0:T(8,128)S(1)}, f32[1,512,128]{2,1,0:T(8,128)S(1)}, u32[]{:S(2)}, u32[]{:S(2)}) collective-permute-start(f32[1,512,128]{2,1,0:T(8,128)S(1)} %get-tuple-element.98), channel_id=1, source_target_pairs={{1,0},{2,1},{3,2},{5,4},{6,5},{7,6},{9,8},{10,9},{11,10},{13,12},{... | collective-permute-start | bytes 786440 | tf_op jit(solution)/shard_map/ppermute | solution.py:20
  376.7 8.7 %collective-permute-start.58 = (f32[1,512,128]{2,1,0:T(8,128)S(1)}, f32[1,512,128]{2,1,0:T(8,128)S(1)}, u32[]{:S(2)}, u32[]{:S(2)}) collective-permute-start(f32[1,512,128]{2,1,0:T(8,128)S(1)} %get-tuple-element.92), channel_id=1, source_target_pairs={{1,0},{2,1},{3,2},{5,4},{6,5},{7,6},{9,8},{10,9},{11,10},{13,12},{... | collective-permute-start | bytes 786440 | tf_op jit(solution)/shard_map/ppermute | solution.py:20
  387.8 8.5 %collective-permute-start.60 = (f32[1,512,128]{2,1,0:T(8,128)S(1)}, f32[1,512,128]{2,1,0:T(8,128)S(1)}, u32[]{:S(2)}, u32[]{:S(2)}) collective-permute-start(f32[1,512,128]{2,1,0:T(8,128)S(1)} %get-tuple-element.90), channel_id=1, source_target_pairs={{1,0},{2,1},{3,2},{5,4},{6,5},{7,6},{9,8},{10,9},{11,10},{13,12},{... | collective-permute-start | bytes 786440 | tf_op jit(solution)/shard_map/ppermute | solution.py:20
  409.4 8.5 %collective-permute-start.64 = (f32[1,512,128]{2,1,0:T(8,128)S(1)}, f32[1,512,128]{2,1,0:T(8,128)S(1)}, u32[]{:S(2)}, u32[]{:S(2)}) collective-permute-start(f32[1,512,128]{2,1,0:T(8,128)S(1)} %get-tuple-element.86), channel_id=1, source_target_pairs={{1,0},{2,1},{3,2},{5,4},{6,5},{7,6},{9,8},{10,9},{11,10},{13,12},{... | collective-permute-start | bytes 786440 | tf_op jit(solution)/shard_map/ppermute | solution.py:20
  420.2 8.5 %collective-permute-start.66 = (f32[1,512,128]{2,1,0:T(8,128)S(1)}, f32[1,512,128]{2,1,0:T(8,128)S(1)}, u32[]{:S(2)}, u32[]{:S(2)}) collective-permute-start(f32[1,512,128]{2,1,0:T(8,128)S(1)} %get-tuple-element.84), channel_id=1, source_target_pairs={{1,0},{2,1},{3,2},{5,4},{6,5},{7,6},{9,8},{10,9},{11,10},{13,12},{... | collective-permute-start | bytes 786440 | tf_op jit(solution)/shard_map/ppermute | solution.py:20
  431.0 8.5 %collective-permute-start.68 = (f32[1,512,128]{2,1,0:T(8,128)S(1)}, f32[1,512,128]{2,1,0:T(8,128)S(1)}, u32[]{:S(2)}, u32[]{:S(2)}) collective-permute-start(f32[1,512,128]{2,1,0:T(8,128)S(1)} %get-tuple-element.82), channel_id=1, source_target_pairs={{1,0},{2,1},{3,2},{5,4},{6,5},{7,6},{9,8},{10,9},{11,10},{13,12},{... | collective-permute-start | bytes 786440 | tf_op jit(solution)/shard_map/ppermute | solution.py:20
  (48 other events, 660.1 us)
Sparse Core Ops, SparseCore 0:
  10.1 51.9 all-gather.1
  455.6 105.8 all-reduce.38
where the time goes:
time: 581 us; the launch traced here: 570 us
  starting transfers between devices  301 us (52%)
  waiting for transfers between devices  199 us (34%)
  other arithmetic  42.4 us (7%)
  between operations  16.7 us (3%)
  local copies, waits for them, and re-layouts  7.08 us (1%)
    ppermute x36, starting transfers between devices, padded_2(): before = lax.ppermute(last, axis, up)  254 us
    unnamed x3, waiting for transfers between devices  105 us
    all_gather x1, waiting for transfers between devices, body(): shard_rows = lax.all_gather(conductivity, 'mesh', axis=1, tiled=True)  54.2 us
    ppermute x36, starting transfers between devices, padded_2(): after = lax.ppermute(leading, axis, down)  46.6 us
    ppermute x36, waiting for transfers between devices, padded_2(): before = lax.ppermute(last, axis, up)  39.3 us
    concatenate x36, other arithmetic, padded_2(): x = jnp.concatenate([before, x, after], axis=dim)  22.2 us
    add x30, other arithmetic, chebyshev(): ratio_next * ratio_now * direct + 2.0 * ratio_next / half_width * remain  15.6 us
  transfers between devices with their start and end apart: 74, of which 38 were waited for; matrix products, arithmetic and copies ran while one was open for 0% of the time, Pallas kernels for 0%

commit v1 on v0

--- a/solution.py
+++ b/solution.py
@@ -7,6 +7,28 @@
 DEG = 6
 low_bound = 0.3
 high_bound = 15.0
+
+
+def joined_along(blocks, dim):
+    blocks = jnp.moveaxis(blocks, 0, dim)
+    lengths = blocks.shape
+    return blocks.reshape(*lengths[:dim], lengths[dim] * lengths[dim + 1], *lengths[dim + 2 :])
+
+
+def grow_blocks(value, axis):
+    size = lax.axis_size(axis)
+    tiles = value[None]
+    for level in range(size.bit_length() - 1):
+        distance = 1 << level
+        other = lax.ppermute(tiles, axis, [(i, i ^ distance) for i in range(size)])
+        both = jnp.stack([tiles, other])
+        upper = lax.axis_index(axis) >> level & 1
+        tiles = jnp.where(upper == 0, both, both[::-1]).reshape(-1, *value.shape)
+    return tiles
+
+
+def collect(array, axis, dim):
+    return joined_along(grow_blocks(array, axis), dim)
 
 
 def padded_2(x, sides, width):
@@ -70,7 +92,7 @@
     tile_count = footprint.shape[1]
     cell_count = depth * block_y * across
     my_blocks = lax.dynamic_index_in_dim(footprint, my_index, 0, keepdims=False)
-    shard_rows = lax.all_gather(conductivity, "mesh", axis=1, tiled=True)
+    shard_rows = collect(conductivity, "mesh", 1)
     row_count = shard_rows.shape[1]
     flat_rows = shard_rows[0].reshape(row_count, cell_count)
     chosen = (my_blocks[:, None] == jnp.arange(row_count, dtype=jnp.int32)[None, :]).astype(

time: 581 us -> 601 us (1.034)
  waiting for transfers between devices: 199 us -> 212 us
    ppermute x0 -> x3, waiting for transfers between devices: none -> 62.1 us  [grow_blocks(): other = lax.ppermute(tiles, axis, [(i, i ^ distance) for i in range(size)])]
    all_gather x1 -> x0, waiting for transfers between devices: 54.2 us -> none  [body(): shard_rows = lax.all_gather(conductivity, 'mesh', axis=1, tiled=True)]
    ppermute x0 -> x3, starting transfers between devices: none -> 7.48 us  [grow_blocks(): other = lax.ppermute(tiles, axis, [(i, i ^ distance) for i in range(size)])]
    unnamed x3 -> x2, waiting for transfers between devices: 105 us -> 107 us
  transfers between devices with their start and end apart: 74 -> 76, of which waited for: 38 -> 40; matrix products, arithmetic and copies ran while one was open for 0% -> 0% of each run, Pallas kernels for 0% -> 0%
where the time goes in v1:
time: 601 us; the launch traced here: 591 us
  starting transfers between devices  307 us (51%)
  waiting for transfers between devices  212 us (35%)
  other arithmetic  44.1 us (7%)
  between operations  16.7 us (3%)
  local copies, waits for them, and re-layouts  7.37 us (1%)
    ppermute x36, starting transfers between devices, padded_2(): before = lax.ppermute(last, axis, up)  252 us
    unnamed x2, waiting for transfers between devices  107 us
    ppermute x3, waiting for transfers between devices, grow_blocks(): other = lax.ppermute(tiles, axis, [(i, i ^ distance) for i in range(size)])  62.1 us
    ppermute x36, starting transfers between devices, padded_2(): after = lax.ppermute(leading, axis, down)  46.6 us
    ppermute x36, waiting for transfers between devices, padded_2(): before = lax.ppermute(last, axis, up)  38.2 us
    concatenate x36, other arithmetic, padded_2(): x = jnp.concatenate([before, x, after], axis=dim)  22.2 us
    add x30, other arithmetic, chebyshev(): ratio_next * ratio_now * direct + 2.0 * ratio_next / half_width * remain  15.6 us
  transfers between devices with their start and end apart: 76, of which 40 were waited for; matrix products, arithmetic and copies ran while one was open for 0% of the time, Pallas kernels for 0%

profile of v1, /device:TPU:0, one launch (start us, length us, event | category | flops | bytes accessed | tf_op | source)
XLA Modules:
  0.0 591.1 jit_solution(5356512839081752207)
XLA Ops:
  19.8 11.3 %collective-permute-done.1 = f32[2,1,4,2,64,128]{5,4,3,2,0,1:T(8,128)S(1)} collective-permute-done((f32[2,1,4,2,64,128]{5,4,3,2,0,1:T(8,128)S(1)}, f32[2,1,4,2,64,128]{5,4,3,2,0,1:T(8,128)S(1)}, u32[]{:S(2)}, u32[]{:S(2)}) %collective-permute-start.1) | collective-permute-done | bytes 524320 | tf_op jit(solution)/shard_map/ppermute | solution.py:23
  33.9 44.3 %collective-permute-done.2 = f32[4,1,4,2,64,128]{5,4,3,2,0,1:T(8,128)S(1)} collective-permute-done((f32[4,1,4,2,64,128]{5,4,3,2,0,1:T(8,128)S(1)}, f32[4,1,4,2,64,128]{5,4,3,2,0,1:T(8,128)S(1)}, u32[]{:S(2)}, u32[]{:S(2)}) %collective-permute-start.2) | collective-permute-done | bytes 1048608 | tf_op jit(solution)/shard_map/ppermute | solution.py:23
  101.3 7.2 %collective-permute-start.8 = (f32[1,512,128]{2,1,0:T(8,128)S(1)}, f32[1,512,128]{2,1,0:T(8,128)S(1)}, u32[]{:S(2)}, u32[]{:S(2)}) collective-permute-start(f32[1,512,128]{2,1,0:T(8,128)S(1)} %get-tuple-element.145), channel_id=1, source_target_pairs={{0,1},{1,2},{2,3},{4,5},{5,6},{6,7},{8,9},{9,10},{10,11},{12,13},{... | collective-permute-start | bytes 786440 | tf_op jit(solution)/shard_map/ppermute | solution.py:41
  125.3 7.3 %collective-permute-start.12 = (f32[1,512,128]{2,1,0:T(8,128)S(1)}, f32[1,512,128]{2,1,0:T(8,128)S(1)}, u32[]{:S(2)}, u32[]{:S(2)}) collective-permute-start(f32[1,512,128]{2,1,0:T(8,128)S(1)} %get-tuple-element.141), channel_id=1, source_target_pairs={{0,1},{1,2},{2,3},{4,5},{5,6},{6,7},{8,9},{9,10},{10,11},{12,13},{... | collective-permute-start | bytes 786440 | tf_op jit(solution)/shard_map/ppermute | solution.py:41
  146.5 7.2 %collective-permute-start.16 = (f32[1,512,128]{2,1,0:T(8,128)S(1)}, f32[1,512,128]{2,1,0:T(8,128)S(1)}, u32[]{:S(2)}, u32[]{:S(2)}) collective-permute-start(f32[1,512,128]{2,1,0:T(8,128)S(1)} %get-tuple-element.137), channel_id=1, source_target_pairs={{0,1},{1,2},{2,3},{4,5},{5,6},{6,7},{8,9},{9,10},{10,11},{12,13},{... | collective-permute-start | bytes 786440 | tf_op jit(solution)/shard_map/ppermute | solution.py:41
  157.3 7.2 %collective-permute-start.18 = (f32[1,512,128]{2,1,0:T(8,128)S(1)}, f32[1,512,128]{2,1,0:T(8,128)S(1)}, u32[]{:S(2)}, u32[]{:S(2)}) collective-permute-start(f32[1,512,128]{2,1,0:T(8,128)S(1)} %get-tuple-element.135), channel_id=1, source_target_pairs={{0,1},{1,2},{2,3},{4,5},{5,6},{6,7},{8,9},{9,10},{10,11},{12,13},{... | collective-permute-start | bytes 786440 | tf_op jit(solution)/shard_map/ppermute | solution.py:41
  168.1 7.2 %collective-permute-start.20 = (f32[1,512,128]{2,1,0:T(8,128)S(1)}, f32[1,512,128]{2,1,0:T(8,128)S(1)}, u32[]{:S(2)}, u32[]{:S(2)}) collective-permute-start(f32[1,512,128]{2,1,0:T(8,128)S(1)} %get-tuple-element.133), channel_id=1, source_target_pairs={{0,1},{1,2},{2,3},{4,5},{5,6},{6,7},{8,9},{9,10},{10,11},{12,13},{... | collective-permute-start | bytes 786440 | tf_op jit(solution)/shard_map/ppermute | solution.py:41
  179.0 7.2 %collective-permute-start.22 = (f32[1,512,128]{2,1,0:T(8,128)S(1)}, f32[1,512,128]{2,1,0:T(8,128)S(1)}, u32[]{:S(2)}, u32[]{:S(2)}) collective-permute-start(f32[1,512,128]{2,1,0:T(8,128)S(1)} %get-tuple-element.131), channel_id=1, source_target_pairs={{0,1},{1,2},{2,3},{4,5},{5,6},{6,7},{8,9},{9,10},{10,11},{12,13},{... | collective-permute-start | bytes 786440 | tf_op jit(solution)/shard_map/ppermute | solution.py:41
  189.8 7.2 %collective-permute-start.24 = (f32[1,512,128]{2,1,0:T(8,128)S(1)}, f32[1,512,128]{2,1,0:T(8,128)S(1)}, u32[]{:S(2)}, u32[]{:S(2)}) collective-permute-start(f32[1,512,128]{2,1,0:T(8,128)S(1)} %get-tuple-element.129), channel_id=1, source_target_pairs={{0,1},{1,2},{2,3},{4,5},{5,6},{6,7},{8,9},{9,10},{10,11},{12,13},{... | collective-permute-start | bytes 786440 | tf_op jit(solution)/shard_map/ppermute | solution.py:41
  200.6 7.2 %collective-permute-start.26 = (f32[1,512,128]{2,1,0:T(8,128)S(1)}, f32[1,512,128]{2,1,0:T(8,128)S(1)}, u32[]{:S(2)}, u32[]{:S(2)}) collective-permute-start(f32[1,512,128]{2,1,0:T(8,128)S(1)} %get-tuple-element.127), channel_id=1, source_target_pairs={{0,1},{1,2},{2,3},{4,5},{5,6},{6,7},{8,9},{9,10},{10,11},{12,13},{... | collective-permute-start | bytes 786440 | tf_op jit(solution)/shard_map/ppermute | solution.py:41
  211.6 7.2 %collective-permute-start.28 = (f32[1,512,128]{2,1,0:T(8,128)S(1)}, f32[1,512,128]{2,1,0:T(8,128)S(1)}, u32[]{:S(2)}, u32[]{:S(2)}) collective-permute-start(f32[1,512,128]{2,1,0:T(8,128)S(1)} %get-tuple-element.125), channel_id=1, source_target_pairs={{0,1},{1,2},{2,3},{4,5},{5,6},{6,7},{8,9},{9,10},{10,11},{12,13},{... | collective-permute-start | bytes 786440 | tf_op jit(solution)/shard_map/ppermute | solution.py:41
  222.4 7.4 %collective-permute-start.30 = (f32[1,512,128]{2,1,0:T(8,128)S(1)}, f32[1,512,128]{2,1,0:T(8,128)S(1)}, u32[]{:S(2)}, u32[]{:S(2)}) collective-permute-start(f32[1,512,128]{2,1,0:T(8,128)S(1)} %get-tuple-element.123), channel_id=1, source_target_pairs={{0,1},{1,2},{2,3},{4,5},{5,6},{6,7},{8,9},{9,10},{10,11},{12,13},{... | collective-permute-start | bytes 786440 | tf_op jit(solution)/shard_map/ppermute | solution.py:41
  233.3 7.2 %collective-permute-start.32 = (f32[1,512,128]{2,1,0:T(8,128)S(1)}, f32[1,512,128]{2,1,0:T(8,128)S(1)}, u32[]{:S(2)}, u32[]{:S(2)}) collective-permute-start(f32[1,512,128]{2,1,0:T(8,128)S(1)} %get-tuple-element.121), channel_id=1, source_target_pairs={{0,1},{1,2},{2,3},{4,5},{5,6},{6,7},{8,9},{9,10},{10,11},{12,13},{... | collective-permute-start | bytes 786440 | tf_op jit(solution)/shard_map/ppermute | solution.py:41
  244.1 7.2 %collective-permute-start.34 = (f32[1,512,128]{2,1,0:T(8,128)S(1)}, f32[1,512,128]{2,1,0:T(8,128)S(1)}, u32[]{:S(2)}, u32[]{:S(2)}) collective-permute-start(f32[1,512,128]{2,1,0:T(8,128)S(1)} %get-tuple-element.119), channel_id=1, source_target_pairs={{0,1},{1,2},{2,3},{4,5},{5,6},{6,7},{8,9},{9,10},{10,11},{12,13},{... | collective-permute-start | bytes 786440 | tf_op jit(solution)/shard_map/ppermute | solution.py:41
  254.9 7.2 %collective-permute-start.36 = (f32[1,512,128]{2,1,0:T(8,128)S(1)}, f32[1,512,128]{2,1,0:T(8,128)S(1)}, u32[]{:S(2)}, u32[]{:S(2)}) collective-permute-start(f32[1,512,128]{2,1,0:T(8,128)S(1)} %get-tuple-element.117), channel_id=1, source_target_pairs={{0,1},{1,2},{2,3},{4,5},{5,6},{6,7},{8,9},{9,10},{10,11},{12,13},{... | collective-permute-start | bytes 786440 | tf_op jit(solution)/shard_map/ppermute | solution.py:41
  265.8 7.2 %collective-permute-start.38 = (f32[1,512,128]{2,1,0:T(8,128)S(1)}, f32[1,512,128]{2,1,0:T(8,128)S(1)}, u32[]{:S(2)}, u32[]{:S(2)}) collective-permute-start(f32[1,512,128]{2,1,0:T(8,128)S(1)} %get-tuple-element.115), channel_id=1, source_target_pairs={{0,1},{1,2},{2,3},{4,5},{5,6},{6,7},{8,9},{9,10},{10,11},{12,13},{... | collective-permute-start | bytes 786440 | tf_op jit(solution)/shard_map/ppermute | solution.py:41
  276.9 7.2 %collective-permute-start.40 = (f32[1,512,128]{2,1,0:T(8,128)S(1)}, f32[1,512,128]{2,1,0:T(8,128)S(1)}, u32[]{:S(2)}, u32[]{:S(2)}) collective-permute-start(f32[1,512,128]{2,1,0:T(8,128)S(1)} %get-tuple-element.113), channel_id=1, source_target_pairs={{0,1},{1,2},{2,3},{4,5},{5,6},{6,7},{8,9},{9,10},{10,11},{12,13},{... | collective-permute-start | bytes 786440 | tf_op jit(solution)/shard_map/ppermute | solution.py:41
  287.7 7.2 %collective-permute-start.42 = (f32[1,512,128]{2,1,0:T(8,128)S(1)}, f32[1,512,128]{2,1,0:T(8,128)S(1)}, u32[]{:S(2)}, u32[]{:S(2)}) collective-permute-start(f32[1,512,128]{2,1,0:T(8,128)S(1)} %get-tuple-element.111), channel_id=1, source_target_pairs={{0,1},{1,2},{2,3},{4,5},{5,6},{6,7},{8,9},{9,10},{10,11},{12,13},{... | collective-permute-start | bytes 786440 | tf_op jit(solution)/shard_map/ppermute | solution.py:41
  298.5 7.2 %collective-permute-start.44 = (f32[1,512,128]{2,1,0:T(8,128)S(1)}, f32[1,512,128]{2,1,0:T(8,128)S(1)}, u32[]{:S(2)}, u32[]{:S(2)}) collective-permute-start(f32[1,512,128]{2,1,0:T(8,128)S(1)} %get-tuple-element.109), channel_id=1, source_target_pairs={{0,1},{1,2},{2,3},{4,5},{5,6},{6,7},{8,9},{9,10},{10,11},{12,13},{... | collective-permute-start | bytes 786440 | tf_op jit(solution)/shard_map/ppermute | solution.py:41
  309.3 7.6 %collective-permute-start.46 = (f32[1,512,128]{2,1,0:T(8,128)S(1)}, f32[1,512,128]{2,1,0:T(8,128)S(1)}, u32[]{:S(2)}, u32[]{:S(2)}) collective-permute-start(f32[1,512,128]{2,1,0:T(8,128)S(1)} %get-tuple-element.107), channel_id=1, source_target_pairs={{0,1},{1,2},{2,3},{4,5},{5,6},{6,7},{8,9},{9,10},{10,11},{12,13},{... | collective-permute-start | bytes 786440 | tf_op jit(solution)/shard_map/ppermute | solution.py:41
  320.1 7.2 %collective-permute-start.48 = (f32[1,512,128]{2,1,0:T(8,128)S(1)}, f32[1,512,128]{2,1,0:T(8,128)S(1)}, u32[]{:S(2)}, u32[]{:S(2)}) collective-permute-start(f32[1,512,128]{2,1,0:T(8,128)S(1)} %get-tuple-element.105), channel_id=1, source_target_pairs={{0,1},{1,2},{2,3},{4,5},{5,6},{6,7},{8,9},{9,10},{10,11},{12,13},{... | collective-permute-start | bytes 786440 | tf_op jit(solution)/shard_map/ppermute | solution.py:41
  330.9 7.2 %collective-permute-start.50 = (f32[1,512,128]{2,1,0:T(8,128)S(1)}, f32[1,512,128]{2,1,0:T(8,128)S(1)}, u32[]{:S(2)}, u32[]{:S(2)}) collective-permute-start(f32[1,512,128]{2,1,0:T(8,128)S(1)} %get-tuple-element.103), channel_id=1, source_target_pairs={{0,1},{1,2},{2,3},{4,5},{5,6},{6,7},{8,9},{9,10},{10,11},{12,13},{... | collective-permute-start | bytes 786440 | tf_op jit(solution)/shard_map/ppermute | solution.py:41
  342.0 7.2 %collective-permute-start.52 = (f32[1,512,128]{2,1,0:T(8,128)S(1)}, f32[1,512,128]{2,1,0:T(8,128)S(1)}, u32[]{:S(2)}, u32[]{:S(2)}) collective-permute-start(f32[1,512,128]{2,1,0:T(8,128)S(1)} %get-tuple-element.101), channel_id=1, source_target_pairs={{0,1},{1,2},{2,3},{4,5},{5,6},{6,7},{8,9},{9,10},{10,11},{12,13},{... | collective-permute-start | bytes 786440 | tf_op jit(solution)/shard_map/ppermute | solution.py:41
  352.8 7.2 %collective-permute-start.54 = (f32[1,512,128]{2,1,0:T(8,128)S(1)}, f32[1,512,128]{2,1,0:T(8,128)S(1)}, u32[]{:S(2)}, u32[]{:S(2)}) collective-permute-start(f32[1,512,128]{2,1,0:T(8,128)S(1)} %get-tuple-element.99), channel_id=1, source_target_pairs={{0,1},{1,2},{2,3},{4,5},{5,6},{6,7},{8,9},{9,10},{10,11},{12,13},{... | collective-permute-start | bytes 786440 | tf_op jit(solution)/shard_map/ppermute | solution.py:41
  363.6 7.2 %collective-permute-start.56 = (f32[1,512,128]{2,1,0:T(8,128)S(1)}, f32[1,512,128]{2,1,0:T(8,128)S(1)}, u32[]{:S(2)}, u32[]{:S(2)}) collective-permute-start(f32[1,512,128]{2,1,0:T(8,128)S(1)} %get-tuple-element.97), channel_id=1, source_target_pairs={{0,1},{1,2},{2,3},{4,5},{5,6},{6,7},{8,9},{9,10},{10,11},{12,13},{... | collective-permute-start | bytes 786440 | tf_op jit(solution)/shard_map/ppermute | solution.py:41
  374.5 7.2 %collective-permute-start.58 = (f32[1,512,128]{2,1,0:T(8,128)S(1)}, f32[1,512,128]{2,1,0:T(8,128)S(1)}, u32[]{:S(2)}, u32[]{:S(2)}) collective-permute-start(f32[1,512,128]{2,1,0:T(8,128)S(1)} %get-tuple-element.95), channel_id=1, source_target_pairs={{0,1},{1,2},{2,3},{4,5},{5,6},{6,7},{8,9},{9,10},{10,11},{12,13},{... | collective-permute-start | bytes 786440 | tf_op jit(solution)/shard_map/ppermute | solution.py:41
  385.3 7.2 %collective-permute-start.60 = (f32[1,512,128]{2,1,0:T(8,128)S(1)}, f32[1,512,128]{2,1,0:T(8,128)S(1)}, u32[]{:S(2)}, u32[]{:S(2)}) collective-permute-start(f32[1,512,128]{2,1,0:T(8,128)S(1)} %get-tuple-element.93), channel_id=1, source_target_pairs={{0,1},{1,2},{2,3},{4,5},{5,6},{6,7},{8,9},{9,10},{10,11},{12,13},{... | collective-permute-start | bytes 786440 | tf_op jit(solution)/shard_map/ppermute | solution.py:41
  396.1 7.4 %collective-permute-start.62 = (f32[1,512,128]{2,1,0:T(8,128)S(1)}, f32[1,512,128]{2,1,0:T(8,128)S(1)}, u32[]{:S(2)}, u32[]{:S(2)}) collective-permute-start(f32[1,512,128]{2,1,0:T(8,128)S(1)} %get-tuple-element.91), channel_id=1, source_target_pairs={{0,1},{1,2},{2,3},{4,5},{5,6},{6,7},{8,9},{9,10},{10,11},{12,13},{... | collective-permute-start | bytes 786440 | tf_op jit(solution)/shard_map/ppermute | solution.py:41
  407.1 7.2 %collective-permute-start.64 = (f32[1,512,128]{2,1,0:T(8,128)S(1)}, f32[1,512,128]{2,1,0:T(8,128)S(1)}, u32[]{:S(2)}, u32[]{:S(2)}) collective-permute-start(f32[1,512,128]{2,1,0:T(8,128)S(1)} %get-tuple-element.89), channel_id=1, source_target_pairs={{0,1},{1,2},{2,3},{4,5},{5,6},{6,7},{8,9},{9,10},{10,11},{12,13},{... | collective-permute-start | bytes 786440 | tf_op jit(solution)/shard_map/ppermute | solution.py:41
  417.9 7.2 %collective-permute-start.66 = (f32[1,512,128]{2,1,0:T(8,128)S(1)}, f32[1,512,128]{2,1,0:T(8,128)S(1)}, u32[]{:S(2)}, u32[]{:S(2)}) collective-permute-start(f32[1,512,128]{2,1,0:T(8,128)S(1)} %get-tuple-element.87), channel_id=1, source_target_pairs={{0,1},{1,2},{2,3},{4,5},{5,6},{6,7},{8,9},{9,10},{10,11},{12,13},{... | collective-permute-start | bytes 786440 | tf_op jit(solution)/shard_map/ppermute | solution.py:41
  428.7 7.2 %collective-permute-start.68 = (f32[1,512,128]{2,1,0:T(8,128)S(1)}, f32[1,512,128]{2,1,0:T(8,128)S(1)}, u32[]{:S(2)}, u32[]{:S(2)}) collective-permute-start(f32[1,512,128]{2,1,0:T(8,128)S(1)} %get-tuple-element.85), channel_id=1, source_target_pairs={{0,1},{1,2},{2,3},{4,5},{5,6},{6,7},{8,9},{9,10},{10,11},{12,13},{... | collective-permute-start | bytes 786440 | tf_op jit(solution)/shard_map/ppermute | solution.py:41
  474.8 107.5 %all-reduce.39.cloned.1.call-done = f32[32,16384]{1,0:T(8,128)} async-done(((f32[32,16384]{1,0:T(8,128)}), f32[32,16384]{1,0:T(8,128)}) %all-reduce.39.cloned.1.call-update) | async-done | bytes 2097168
  (258 shorter events, 202.2 us)
Async XLA Ops:
  7.2 575.1 %all-reduce.39.cloned.1.call-start = ((), (), s32[]{:S(2)}) async-start(), calls=%async_computation | async-start | bytes 4194304
  7.2 9.5 %collective-permute-start = (f32[1,1,4,2,64,128]{5,4,3,2,1,0:T(8,128)}, f32[1,1,4,2,64,128]{5,4,3,2,1,0:T(8,128)S(1)}, u32[]{:S(2)}, u32[]{:S(2)}) collective-permute-start(f32[1,1,4,2,64,128]{5,4,3,2,1,0:T(8,128)} %bitcast.201), channel_id=1, source_target_pairs={{0,4},{4,0},{8,12},{12,8},{16,20},{20,16},{24,28},{28,24},{1,5},{5... | collective-permute-start | bytes 786440 | tf_op jit(solution)/shard_map/ppermute | solution.py:23
  17.9 13.2 %collective-permute-start.1 = (f32[2,1,4,2,64,128]{5,4,3,2,0,1:T(8,128)S(1)}, f32[2,1,4,2,64,128]{5,4,3,2,0,1:T(8,128)S(1)}, u32[]{:S(2)}, u32[]{:S(2)}) collective-permute-start(f32[2,1,4,2,64,128]{5,4,3,2,0,1:T(8,128)S(1)} %get-tuple-element.152), channel_id=1, source_target_pairs={{0,8},{4,12},{8,0},{12,4},{16,24},{20,28},{24,16},{28,20},{1,9},{5... | collective-permute-start | bytes 1572872 | tf_op jit(solution)/shard_map/ppermute | solution.py:23
  31.3 46.9 %collective-permute-start.2 = (f32[4,1,4,2,64,128]{5,4,3,2,0,1:T(8,128)S(1)}, f32[4,1,4,2,64,128]{5,4,3,2,0,1:T(8,128)S(1)}, u32[]{:S(2)}, u32[]{:S(2)}) collective-permute-start(f32[4,1,4,2,64,128]{5,4,3,2,0,1:T(8,128)S(1)} %bitcast.193), channel_id=1, source_target_pairs={{0,16},{4,20},{8,24},{12,28},{16,0},{20,4},{24,8},{28,12},{1,17},{... | collective-permute-start | bytes 3145736 | tf_op jit(solution)/shard_map/ppermute | solution.py:23
  100.0 8.5 %collective-permute-start.7 = (f32[1,512,128]{2,1,0:T(8,128)S(1)}, f32[1,512,128]{2,1,0:T(8,128)S(1)}, u32[]{:S(2)}, u32[]{:S(2)}) collective-permute-start(f32[1,512,128]{2,1,0:T(8,128)S(1)} %get-tuple-element.146), channel_id=1, source_target_pairs={{1,0},{2,1},{3,2},{5,4},{6,5},{7,6},{9,8},{10,9},{11,10},{13,12},{... | collective-permute-start | bytes 786440 | tf_op jit(solution)/shard_map/ppermute | solution.py:42
  124.0 8.6 %collective-permute-start.11 = (f32[1,512,128]{2,1,0:T(8,128)S(1)}, f32[1,512,128]{2,1,0:T(8,128)S(1)}, u32[]{:S(2)}, u32[]{:S(2)}) collective-permute-start(f32[1,512,128]{2,1,0:T(8,128)S(1)} %get-tuple-element.142), channel_id=1, source_target_pairs={{1,0},{2,1},{3,2},{5,4},{6,5},{7,6},{9,8},{10,9},{11,10},{13,12},{... | collective-permute-start | bytes 786440 | tf_op jit(solution)/shard_map/ppermute | solution.py:42
  145.2 8.5 %collective-permute-start.15 = (f32[1,512,128]{2,1,0:T(8,128)S(1)}, f32[1,512,128]{2,1,0:T(8,128)S(1)}, u32[]{:S(2)}, u32[]{:S(2)}) collective-permute-start(f32[1,512,128]{2,1,0:T(8,128)S(1)} %get-tuple-element.138), channel_id=1, source_target_pairs={{1,0},{2,1},{3,2},{5,4},{6,5},{7,6},{9,8},{10,9},{11,10},{13,12},{... | collective-permute-start | bytes 786440 | tf_op jit(solution)/shard_map/ppermute | solution.py:42
  156.0 8.5 %collective-permute-start.17 = (f32[1,512,128]{2,1,0:T(8,128)S(1)}, f32[1,512,128]{2,1,0:T(8,128)S(1)}, u32[]{:S(2)}, u32[]{:S(2)}) collective-permute-start(f32[1,512,128]{2,1,0:T(8,128)S(1)} %get-tuple-element.136), channel_id=1, source_target_pairs={{1,0},{2,1},{3,2},{5,4},{6,5},{7,6},{9,8},{10,9},{11,10},{13,12},{... | collective-permute-start | bytes 786440 | tf_op jit(solution)/shard_map/ppermute | solution.py:42
  166.8 8.5 %collective-permute-start.19 = (f32[1,512,128]{2,1,0:T(8,128)S(1)}, f32[1,512,128]{2,1,0:T(8,128)S(1)}, u32[]{:S(2)}, u32[]{:S(2)}) collective-permute-start(f32[1,512,128]{2,1,0:T(8,128)S(1)} %get-tuple-element.134), channel_id=1, source_target_pairs={{1,0},{2,1},{3,2},{5,4},{6,5},{7,6},{9,8},{10,9},{11,10},{13,12},{... | collective-permute-start | bytes 786440 | tf_op jit(solution)/shard_map/ppermute | solution.py:42
  177.7 8.5 %collective-permute-start.21 = (f32[1,512,128]{2,1,0:T(8,128)S(1)}, f32[1,512,128]{2,1,0:T(8,128)S(1)}, u32[]{:S(2)}, u32[]{:S(2)}) collective-permute-start(f32[1,512,128]{2,1,0:T(8,128)S(1)} %get-tuple-element.132), channel_id=1, source_target_pairs={{1,0},{2,1},{3,2},{5,4},{6,5},{7,6},{9,8},{10,9},{11,10},{13,12},{... | collective-permute-start | bytes 786440 | tf_op jit(solution)/shard_map/ppermute | solution.py:42
  188.5 8.5 %collective-permute-start.23 = (f32[1,512,128]{2,1,0:T(8,128)S(1)}, f32[1,512,128]{2,1,0:T(8,128)S(1)}, u32[]{:S(2)}, u32[]{:S(2)}) collective-permute-start(f32[1,512,128]{2,1,0:T(8,128)S(1)} %get-tuple-element.130), channel_id=1, source_target_pairs={{1,0},{2,1},{3,2},{5,4},{6,5},{7,6},{9,8},{10,9},{11,10},{13,12},{... | collective-permute-start | bytes 786440 | tf_op jit(solution)/shard_map/ppermute | solution.py:42
  199.3 8.5 %collective-permute-start.25 = (f32[1,512,128]{2,1,0:T(8,128)S(1)}, f32[1,512,128]{2,1,0:T(8,128)S(1)}, u32[]{:S(2)}, u32[]{:S(2)}) collective-permute-start(f32[1,512,128]{2,1,0:T(8,128)S(1)} %get-tuple-element.128), channel_id=1, source_target_pairs={{1,0},{2,1},{3,2},{5,4},{6,5},{7,6},{9,8},{10,9},{11,10},{13,12},{... | collective-permute-start | bytes 786440 | tf_op jit(solution)/shard_map/ppermute | solution.py:42
  210.3 8.5 %collective-permute-start.27 = (f32[1,512,128]{2,1,0:T(8,128)S(1)}, f32[1,512,128]{2,1,0:T(8,128)S(1)}, u32[]{:S(2)}, u32[]{:S(2)}) collective-permute-start(f32[1,512,128]{2,1,0:T(8,128)S(1)} %get-tuple-element.126), channel_id=1, source_target_pairs={{1,0},{2,1},{3,2},{5,4},{6,5},{7,6},{9,8},{10,9},{11,10},{13,12},{... | collective-permute-start | bytes 786440 | tf_op jit(solution)/shard_map/ppermute | solution.py:42
  221.1 8.7 %collective-permute-start.29 = (f32[1,512,128]{2,1,0:T(8,128)S(1)}, f32[1,512,128]{2,1,0:T(8,128)S(1)}, u32[]{:S(2)}, u32[]{:S(2)}) collective-permute-start(f32[1,512,128]{2,1,0:T(8,128)S(1)} %get-tuple-element.124), channel_id=1, source_target_pairs={{1,0},{2,1},{3,2},{5,4},{6,5},{7,6},{9,8},{10,9},{11,10},{13,12},{... | collective-permute-start | bytes 786440 | tf_op jit(solution)/shard_map/ppermute | solution.py:42
  232.0 8.5 %collective-permute-start.31 = (f32[1,512,128]{2,1,0:T(8,128)S(1)}, f32[1,512,128]{2,1,0:T(8,128)S(1)}, u32[]{:S(2)}, u32[]{:S(2)}) collective-permute-start(f32[1,512,128]{2,1,0:T(8,128)S(1)} %get-tuple-element.122), channel_id=1, source_target_pairs={{1,0},{2,1},{3,2},{5,4},{6,5},{7,6},{9,8},{10,9},{11,10},{13,12},{... | collective-permute-start | bytes 786440 | tf_op jit(solution)/shard_map/ppermute | solution.py:42
  242.8 8.5 %collective-permute-start.33 = (f32[1,512,128]{2,1,0:T(8,128)S(1)}, f32[1,512,128]{2,1,0:T(8,128)S(1)}, u32[]{:S(2)}, u32[]{:S(2)}) collective-permute-start(f32[1,512,128]{2,1,0:T(8,128)S(1)} %get-tuple-element.120), channel_id=1, source_target_pairs={{1,0},{2,1},{3,2},{5,4},{6,5},{7,6},{9,8},{10,9},{11,10},{13,12},{... | collective-permute-start | bytes 786440 | tf_op jit(solution)/shard_map/ppermute | solution.py:42
  253.6 8.5 %collective-permute-start.35 = (f32[1,512,128]{2,1,0:T(8,128)S(1)}, f32[1,512,128]{2,1,0:T(8,128)S(1)}, u32[]{:S(2)}, u32[]{:S(2)}) collective-permute-start(f32[1,512,128]{2,1,0:T(8,128)S(1)} %get-tuple-element.118), channel_id=1, source_target_pairs={{1,0},{2,1},{3,2},{5,4},{6,5},{7,6},{9,8},{10,9},{11,10},{13,12},{... | collective-permute-start | bytes 786440 | tf_op jit(solution)/shard_map/ppermute | solution.py:42
  264.4 8.6 %collective-permute-start.37 = (f32[1,512,128]{2,1,0:T(8,128)S(1)}, f32[1,512,128]{2,1,0:T(8,128)S(1)}, u32[]{:S(2)}, u32[]{:S(2)}) collective-permute-start(f32[1,512,128]{2,1,0:T(8,128)S(1)} %get-tuple-element.116), channel_id=1, source_target_pairs={{1,0},{2,1},{3,2},{5,4},{6,5},{7,6},{9,8},{10,9},{11,10},{13,12},{... | collective-permute-start | bytes 786440 | tf_op jit(solution)/shard_map/ppermute | solution.py:42
  275.6 8.5 %collective-permute-start.39 = (f32[1,512,128]{2,1,0:T(8,128)S(1)}, f32[1,512,128]{2,1,0:T(8,128)S(1)}, u32[]{:S(2)}, u32[]{:S(2)}) collective-permute-start(f32[1,512,128]{2,1,0:T(8,128)S(1)} %get-tuple-element.114), channel_id=1, source_target_pairs={{1,0},{2,1},{3,2},{5,4},{6,5},{7,6},{9,8},{10,9},{11,10},{13,12},{... | collective-permute-start | bytes 786440 | tf_op jit(solution)/shard_map/ppermute | solution.py:42
  286.4 8.5 %collective-permute-start.41 = (f32[1,512,128]{2,1,0:T(8,128)S(1)}, f32[1,512,128]{2,1,0:T(8,128)S(1)}, u32[]{:S(2)}, u32[]{:S(2)}) collective-permute-start(f32[1,512,128]{2,1,0:T(8,128)S(1)} %get-tuple-element.112), channel_id=1, source_target_pairs={{1,0},{2,1},{3,2},{5,4},{6,5},{7,6},{9,8},{10,9},{11,10},{13,12},{... | collective-permute-start | bytes 786440 | tf_op jit(solution)/shard_map/ppermute | solution.py:42
  297.2 8.5 %collective-permute-start.43 = (f32[1,512,128]{2,1,0:T(8,128)S(1)}, f32[1,512,128]{2,1,0:T(8,128)S(1)}, u32[]{:S(2)}, u32[]{:S(2)}) collective-permute-start(f32[1,512,128]{2,1,0:T(8,128)S(1)} %get-tuple-element.110), channel_id=1, source_target_pairs={{1,0},{2,1},{3,2},{5,4},{6,5},{7,6},{9,8},{10,9},{11,10},{13,12},{... | collective-permute-start | bytes 786440 | tf_op jit(solution)/shard_map/ppermute | solution.py:42
  308.0 8.9 %collective-permute-start.45 = (f32[1,512,128]{2,1,0:T(8,128)S(1)}, f32[1,512,128]{2,1,0:T(8,128)S(1)}, u32[]{:S(2)}, u32[]{:S(2)}) collective-permute-start(f32[1,512,128]{2,1,0:T(8,128)S(1)} %get-tuple-element.108), channel_id=1, source_target_pairs={{1,0},{2,1},{3,2},{5,4},{6,5},{7,6},{9,8},{10,9},{11,10},{13,12},{... | collective-permute-start | bytes 786440 | tf_op jit(solution)/shard_map/ppermute | solution.py:42
  318.8 8.5 %collective-permute-start.47 = (f32[1,512,128]{2,1,0:T(8,128)S(1)}, f32[1,512,128]{2,1,0:T(8,128)S(1)}, u32[]{:S(2)}, u32[]{:S(2)}) collective-permute-start(f32[1,512,128]{2,1,0:T(8,128)S(1)} %get-tuple-element.106), channel_id=1, source_target_pairs={{1,0},{2,1},{3,2},{5,4},{6,5},{7,6},{9,8},{10,9},{11,10},{13,12},{... | collective-permute-start | bytes 786440 | tf_op jit(solution)/shard_map/ppermute | solution.py:42
  329.6 8.5 %collective-permute-start.49 = (f32[1,512,128]{2,1,0:T(8,128)S(1)}, f32[1,512,128]{2,1,0:T(8,128)S(1)}, u32[]{:S(2)}, u32[]{:S(2)}) collective-permute-start(f32[1,512,128]{2,1,0:T(8,128)S(1)} %get-tuple-element.104), channel_id=1, source_target_pairs={{1,0},{2,1},{3,2},{5,4},{6,5},{7,6},{9,8},{10,9},{11,10},{13,12},{... | collective-permute-start | bytes 786440 | tf_op jit(solution)/shard_map/ppermute | solution.py:42
  340.7 8.5 %collective-permute-start.51 = (f32[1,512,128]{2,1,0:T(8,128)S(1)}, f32[1,512,128]{2,1,0:T(8,128)S(1)}, u32[]{:S(2)}, u32[]{:S(2)}) collective-permute-start(f32[1,512,128]{2,1,0:T(8,128)S(1)} %get-tuple-element.102), channel_id=1, source_target_pairs={{1,0},{2,1},{3,2},{5,4},{6,5},{7,6},{9,8},{10,9},{11,10},{13,12},{... | collective-permute-start | bytes 786440 | tf_op jit(solution)/shard_map/ppermute | solution.py:42
  351.5 8.5 %collective-permute-start.53 = (f32[1,512,128]{2,1,0:T(8,128)S(1)}, f32[1,512,128]{2,1,0:T(8,128)S(1)}, u32[]{:S(2)}, u32[]{:S(2)}) collective-permute-start(f32[1,512,128]{2,1,0:T(8,128)S(1)} %get-tuple-element.100), channel_id=1, source_target_pairs={{1,0},{2,1},{3,2},{5,4},{6,5},{7,6},{9,8},{10,9},{11,10},{13,12},{... | collective-permute-start | bytes 786440 | tf_op jit(solution)/shard_map/ppermute | solution.py:42
  362.3 8.5 %collective-permute-start.55 = (f32[1,512,128]{2,1,0:T(8,128)S(1)}, f32[1,512,128]{2,1,0:T(8,128)S(1)}, u32[]{:S(2)}, u32[]{:S(2)}) collective-permute-start(f32[1,512,128]{2,1,0:T(8,128)S(1)} %get-tuple-element.98), channel_id=1, source_target_pairs={{1,0},{2,1},{3,2},{5,4},{6,5},{7,6},{9,8},{10,9},{11,10},{13,12},{... | collective-permute-start | bytes 786440 | tf_op jit(solution)/shard_map/ppermute | solution.py:42
  373.2 8.5 %collective-permute-start.57 = (f32[1,512,128]{2,1,0:T(8,128)S(1)}, f32[1,512,128]{2,1,0:T(8,128)S(1)}, u32[]{:S(2)}, u32[]{:S(2)}) collective-permute-start(f32[1,512,128]{2,1,0:T(8,128)S(1)} %get-tuple-element.96), channel_id=1, source_target_pairs={{1,0},{2,1},{3,2},{5,4},{6,5},{7,6},{9,8},{10,9},{11,10},{13,12},{... | collective-permute-start | bytes 786440 | tf_op jit(solution)/shard_map/ppermute | solution.py:42
  384.0 8.5 %collective-permute-start.59 = (f32[1,512,128]{2,1,0:T(8,128)S(1)}, f32[1,512,128]{2,1,0:T(8,128)S(1)}, u32[]{:S(2)}, u32[]{:S(2)}) collective-permute-start(f32[1,512,128]{2,1,0:T(8,128)S(1)} %get-tuple-element.94), channel_id=1, source_target_pairs={{1,0},{2,1},{3,2},{5,4},{6,5},{7,6},{9,8},{10,9},{11,10},{13,12},{... | collective-permute-start | bytes 786440 | tf_op jit(solution)/shard_map/ppermute | solution.py:42
  394.8 8.7 %collective-permute-start.61 = (f32[1,512,128]{2,1,0:T(8,128)S(1)}, f32[1,512,128]{2,1,0:T(8,128)S(1)}, u32[]{:S(2)}, u32[]{:S(2)}) collective-permute-start(f32[1,512,128]{2,1,0:T(8,128)S(1)} %get-tuple-element.92), channel_id=1, source_target_pairs={{1,0},{2,1},{3,2},{5,4},{6,5},{7,6},{9,8},{10,9},{11,10},{13,12},{... | collective-permute-start | bytes 786440 | tf_op jit(solution)/shard_map/ppermute | solution.py:42
  416.6 8.5 %collective-permute-start.65 = (f32[1,512,128]{2,1,0:T(8,128)S(1)}, f32[1,512,128]{2,1,0:T(8,128)S(1)}, u32[]{:S(2)}, u32[]{:S(2)}) collective-permute-start(f32[1,512,128]{2,1,0:T(8,128)S(1)} %get-tuple-element.88), channel_id=1, source_target_pairs={{1,0},{2,1},{3,2},{5,4},{6,5},{7,6},{9,8},{10,9},{11,10},{13,12},{... | collective-permute-start | bytes 786440 | tf_op jit(solution)/shard_map/ppermute | solution.py:42
  427.4 8.5 %collective-permute-start.67 = (f32[1,512,128]{2,1,0:T(8,128)S(1)}, f32[1,512,128]{2,1,0:T(8,128)S(1)}, u32[]{:S(2)}, u32[]{:S(2)}) collective-permute-start(f32[1,512,128]{2,1,0:T(8,128)S(1)} %get-tuple-element.86), channel_id=1, source_target_pairs={{1,0},{2,1},{3,2},{5,4},{6,5},{7,6},{9,8},{10,9},{11,10},{13,12},{... | collective-permute-start | bytes 786440 | tf_op jit(solution)/shard_map/ppermute | solution.py:42
  (50 other events, 700.3 us)
Sparse Core Ops, SparseCore 0:
  473.7 108.5 all-reduce.38
